TPU v7x, 128 devices: a whole 4x4x4 slice. The times are simulated.
128 devices in a mesh: row: 8 (over y_lo, z), col: 16 (over x, y_hi, core).
Axes of the slice: x: 4, y: 4 (y_hi: 2, y_lo: 2; y = y_hi * 2 + y_lo), z: 4, core: 2. Of those that a mesh axis runs over, the one named last changes fastest.
Arguments:
- hessian: float32 [16384, 8, 16, 128], P('row', None, 'col'), may hold values from -1 to 16, as said below
- weights: bfloat16 [512, 16384], P('col', 'row'), may hold values from -6 to 6
- codes: int32 [512, 8192], P('col', 'row'), may hold values from 0 to 255
- tile_map: int32 [32, 64], P('col', 'row'), may hold values from 0 to 511
- codebooks: float32 [512, 2, 256], replicated, may hold values from -6 to 6
Outputs:
- adjusted_codebooks: float32 [512, 2, 256], replicated
Inputs may be any that keep to these rules, and one draw needn't show every extreme that they name: `hessian`: H is symmetric with a dominant positive diagonal.
All inputs are finite; a program needn't handle non-finite values.
Results may differ from a plain program's by a relative error of at most 0.0003.
Values sent between devices are 32-bit elements; how exact they have to be, the bound alone decides.
No kernel may reach another device: no remote copies, remote signals or barrier semaphores. Data moves between devices by JAX's collectives and lax.ppermute only.
A program may use at most 64 MiB of HBM per device.

v0:
```python
import jax
import jax.numpy as jnp
from jax import lax
from jax.sharding import PartitionSpec as P

CODES = 256
NB = 512
TILE_ROWS = 16
TILE_COLS = 256
STEPS = 2
learn_rate = 0.01


def per_device(hessian, weights, codes, tile_map, codebooks):
    rows_local, cols_local = weights.shape
    rows_tiles = rows_local // TILE_ROWS
    cols_tiles = cols_local // TILE_COLS
    tile_count = rows_tiles * cols_tiles
    half_width = TILE_COLS // 2
    pair_count = TILE_ROWS * half_width
    hessian_tile = hessian.reshape(
        hessian.shape[0], hessian.shape[1] * hessian.shape[2] * hessian.shape[3]
    )
    code_tiles = (
        codes.reshape(rows_tiles, TILE_ROWS, cols_tiles, half_width)
        .transpose(0, 2, 1, 3)
        .reshape(tile_count, pair_count)
    )
    code_onehot = (
        code_tiles[:, :, None] == lax.broadcasted_iota(jnp.int32, (1, 1, CODES), 2)
    ).astype(jnp.float32)
    book_onehot = (
        tile_map.reshape(-1)[:, None] == lax.broadcasted_iota(jnp.int32, (1, NB), 1)
    ).astype(jnp.float32)
    for iteration in range(STEPS):
        tile_books = jnp.einsum(
            "tb,bck->tck", book_onehot, codebooks, precision=lax.Precision.HIGHEST
        )
        rebuilt_tiles = jnp.einsum(
            "tpk,tck->tpc", code_onehot, tile_books, precision=lax.Precision.HIGHEST
        )
        rebuilt = (
            rebuilt_tiles.reshape(rows_tiles, cols_tiles, TILE_ROWS, half_width, 2)
            .transpose(0, 2, 1, 3, 4)
            .reshape(rows_local, cols_local)
        )
        error = rebuilt - weights.astype(jnp.float32)
        gathered = lax.all_gather(error, "col", axis=0, tiled=True)
        piece_width = cols_local // lax.axis_size("col")
        error_piece = lax.dynamic_slice_in_dim(
            gathered, lax.axis_index("col") * piece_width, piece_width, 1
        )
        error_spread = lax.all_gather(error_piece, "row", axis=1, tiled=True)
        weight_grad = 2.0 * lax.psum_scatter(
            lax.dot_general(
                error_spread,
                hessian_tile,
                (((1,), (1,)), ((), ())),
                precision=lax.Precision.HIGHEST,
                preferred_element_type=jnp.float32,
            ),
            "col",
            scatter_dimension=0,
            tiled=True,
        )
        grad_tiles = (
            weight_grad.reshape(rows_tiles, TILE_ROWS, cols_tiles, half_width, 2)
            .transpose(0, 2, 1, 3, 4)
            .reshape(tile_count, pair_count, 2)
        )
        tile_grads = jnp.einsum(
            "tpk,tpc->tck", code_onehot, grad_tiles, precision=lax.Precision.HIGHEST
        )
        local_grad = jnp.einsum(
            "tb,tck->bck", book_onehot, tile_grads, precision=lax.Precision.HIGHEST
        )
        total_even, total_odd = lax.psum((local_grad[:, 0, :], local_grad[:, 1, :]), ("row", "col"))
        book_grad = jnp.stack([total_even, total_odd], axis=1)
        codebooks = codebooks - learn_rate * book_grad
    return codebooks


def solution(mesh):
    placed = (P("row", None, "col", None), P("col", "row"), P("col", "row"), P("col", "row"), P())
    return jax.shard_map(per_device, mesh=mesh, in_specs=placed, out_specs=P(), check_vma=False)
```

profile of v0, /device:TPU:1, one launch (start us, length us, event | category | flops | bytes accessed | tf_op | source)
XLA Modules:
  0.0 803.9 jit_solution(11324388309986088203)
XLA Ops:
  8.3 1.7 fusion.16
  10.0 17.1 %fusion.3 = f32[16,2048,2]{1,2,0:T(2,128)S(1)} fusion(s32[16,2048]{1,0:T(8,128)S(1)} %bitcast_bitcast_fusion, f32[16,2,256]{2,0,1:T(8,128)S(1)} %fusion.16), kind=kOutput, calls=%fused_computation.4 | convolution fusion | flops 209715200 | bytes 425984 | tf_op jit(solution)/shard_map/tpk,tck->tpc/dot_general | solution.py:39
  27.3 1.4 copy.39
  28.7 1.1 reshape.34
  31.0 59.7 %all-gather.5.cloned.1.call-done = f32[512,2048]{1,0:T(8,128)} async-done(((f32[32,2048]{1,0:T(8,128)}), f32[512,2048]{1,0:T(8,128)}) %all-gather.5.cloned.1.call-update) | async-done | bytes 4194320 | tf_op jit(solution)/shard_map/all_gather | solution.py:48
  90.7 1.7 constant_dynamic-slice_fusion.1
  92.4 39.8 %all-gather.7.cloned.1.call-done = f32[512,1024]{1,0:T(8,128)} async-done(((f32[512,128]{1,0:T(8,128)}), f32[512,1024]{1,0:T(8,128)}) %all-gather.7.cloned.1.call-update) | async-done | bytes 2097168 | tf_op jit(solution)/shard_map/all_gather | solution.py:53
  132.2 19.4 %fusion.10 = f32[512,2048]{1,0:T(8,128)} fusion(f32[512,1024]{1,0:T(8,128)} %all-gather.7.cloned.1.call-done, f32[256,8,8,128]{3,2,1,0:T(8,128)} %bitcast.51), kind=kOutput, calls=%fused_computation.11 | convolution fusion | flops 12884901888 | bytes 14680064 | tf_op jit(solution)/shard_map/dot_general | solution.py:55
  151.8 84.1 %reduce-scatter.3.cloned.1.call-done = f32[32,2048]{1,0:T(8,128)} async-done(((f32[512,2048]{1,0:T(8,128)}), f32[32,2048]{1,0:T(8,128)}) %reduce-scatter.3.cloned.1.call-update) | async-done | bytes 262160 | tf_op jit(solution)/shard_map/reduce_scatter | solution.py:54
  235.9 1.0 broadcast_multiply_fusion.1
  237.2 1.2 reshape.36
  239.4 12.3 %fusion.2 = f32[16,2,256]{2,1,0:T(2,128)S(1)} fusion(f32[16,2048,2]{1,2,0:T(2,128)S(1)} %reshape.47, s32[16,2048]{1,0:T(8,128)} %copy-done.4), kind=kOutput, calls=%fused_computation.3 | convolution fusion | flops 209715200 | bytes 425984 | tf_op jit(solution)/shard_map/tpk,tpc->tck/dot_general | solution.py:71
  252.4 1.0 fusion.38
  253.5 148.0 %all-reduce.7.cloned.1.call-done = (f32[512,1,256]{2,0,1:T(8,128)}, f32[512,1,256]{2,0,1:T(8,128)}) async-done(((f32[512,1,256]{2,0,1:T(8,128)}, f32[512,1,256]{2,0,1:T(8,128)}), (f32[512,1,256]{2,0,1:T(8,128)}, f32[512,1,256]{2,0,1:T(8,128)})) %all-reduce.7.cloned.1.call-update) | async-done | bytes 1048592 | tf_op jit(solution)/shard_map/psum | solution.py:77
  401.6 1.7 fusion.18
  403.3 17.1 %fusion.1 = f32[16,2048,2]{1,2,0:T(2,128)S(1)} fusion(s32[16,2048]{1,0:T(8,128)S(1)} %copy-done.5, f32[16,2,256]{2,0,1:T(8,128)S(1)} %fusion.18), kind=kOutput, calls=%fused_computation.2 | convolution fusion | flops 209715200 | bytes 425984 | tf_op jit(solution)/shard_map/tpk,tck->tpc/dot_general | solution.py:39
  420.6 1.4 copy.47
  422.0 2.1 reshape.39
  424.1 1.5 copy.48
  426.4 55.1 %all-gather.9.cloned.1.call-done = f32[512,2048]{1,0:T(8,128)} async-done(((f32[32,2048]{1,0:T(8,128)}), f32[512,2048]{1,0:T(8,128)}) %all-gather.9.cloned.1.call-update) | async-done | bytes 4194320 | tf_op jit(solution)/shard_map/all_gather | solution.py:48
  481.6 1.7 constant_dynamic-slice_fusion
  483.6 39.5 %all-gather.11.cloned.1.call-done = f32[512,1024]{1,0:T(8,128)} async-done(((f32[512,128]{1,0:T(8,128)}), f32[512,1024]{1,0:T(8,128)}) %all-gather.11.cloned.1.call-update) | async-done | bytes 2097168 | tf_op jit(solution)/shard_map/all_gather | solution.py:53
  523.1 19.4 %fusion.8 = f32[512,2048]{1,0:T(8,128)} fusion(f32[512,1024]{1,0:T(8,128)} %all-gather.11.cloned.1.call-done, f32[256,8,8,128]{3,2,1,0:T(8,128)} %bitcast.52), kind=kOutput, calls=%fused_computation.9 | convolution fusion | flops 12884901888 | bytes 14680064 | tf_op jit(solution)/shard_map/dot_general | solution.py:55
  542.8 84.0 %reduce-scatter.5.cloned.1.call-done = f32[32,2048]{1,0:T(8,128)} async-done(((f32[512,2048]{1,0:T(8,128)}), f32[32,2048]{1,0:T(8,128)}) %reduce-scatter.5.cloned.1.call-update) | async-done | bytes 262160 | tf_op jit(solution)/shard_map/reduce_scatter | solution.py:54
  626.9 1.0 broadcast_multiply_fusion
  627.8 1.3 copy.49
  629.2 2.5 reshape.40
  632.7 11.3 %fusion = f32[16,2,256]{2,1,0:T(2,128)S(1)} fusion(f32[16,2048,2]{1,2,0:T(2,128)S(1)} %reshape.48, s32[16,2048]{1,0:T(8,128)S(1)} %copy-done.6), kind=kOutput, calls=%fused_computation.1 | convolution fusion | flops 209715200 | bytes 425984 | tf_op jit(solution)/shard_map/tpk,tpc->tck/dot_general | solution.py:71
  644.7 1.0 fusion.37
  645.7 148.1 %all-reduce.5.cloned.1.call-done = (f32[512,1,256]{2,0,1:T(8,128)}, f32[512,1,256]{2,0,1:T(8,128)}) async-done(((f32[512,1,256]{2,0,1:T(8,128)}, f32[512,1,256]{2,0,1:T(8,128)}), (f32[512,1,256]{2,0,1:T(8,128)}, f32[512,1,256]{2,0,1:T(8,128)})) %all-reduce.5.cloned.1.call-update) | async-done | bytes 1048592 | tf_op jit(solution)/shard_map/psum | solution.py:77
  793.9 1.4 fusion.15
  795.3 1.8 copy.53
  (45 shorter events, 8.7 us)
Async XLA Ops:
  6.5 84.1 %all-gather.5.cloned.1.call-start = ((), (), s32[]{:S(2)}) async-start(), calls=%async_computation.2 | async-start | bytes 4456448 | tf_op jit(solution)/shard_map/all_gather | solution.py:48
  8.2 1.7 copy-start.4
  10.0 20.2 %copy-start.3 = (bf16[32,2048]{1,0:T(8,128)(2,1)S(1)}, bf16[32,2048]{1,0:T(8,128)(2,1)}, u32[]{:S(2)}) copy-start(bf16[32,2048]{1,0:T(8,128)(2,1)} %param.6) | copy-start | bytes 393220
  30.9 101.3 %all-gather.7.cloned.1.call-start = ((), (), s32[]{:S(2)}) async-start(), calls=%async_computation.3 | async-start | bytes 2359296 | tf_op jit(solution)/shard_map/all_gather | solution.py:53
  92.4 143.6 %reduce-scatter.3.cloned.1.call-start = ((), (), s32[]{:S(2)}) async-start(), calls=%async_computation.4 | async-start | bytes 4456448 | tf_op jit(solution)/shard_map/reduce_scatter | solution.py:54
  151.6 250.0 %all-reduce.7.cloned.1.call-start = ((), (), s32[]{:S(2)}) async-start(), calls=%async_computation.9 | async-start | bytes 2097152 | tf_op jit(solution)/shard_map/psum | solution.py:77
  239.2 162.3 %copy-start = (f32[512,2,256]{2,1,0:T(2,128)S(1)}, f32[512,2,256]{2,1,0:T(2,128)}, u32[]{:S(2)}) copy-start(f32[512,2,256]{2,1,0:T(2,128)} %param.9) | copy-start | bytes 3145732
  239.4 163.9 %copy-start.5 = (s32[16,2048]{1,0:T(8,128)S(1)}, s32[16,2048]{1,0:T(8,128)}, u32[]{:S(2)}) copy-start(s32[16,2048]{1,0:T(8,128)} %copy-done.4) | copy-start | bytes 393220
  253.5 228.1 %all-gather.9.cloned.1.call-start = ((), (), s32[]{:S(2)}) async-start(), calls=%async_computation.5 | async-start | bytes 4456448 | tf_op jit(solution)/shard_map/all_gather | solution.py:48
  426.4 96.7 %all-gather.11.cloned.1.call-start = ((), (), s32[]{:S(2)}) async-start(), calls=%async_computation.6 | async-start | bytes 2359296 | tf_op jit(solution)/shard_map/all_gather | solution.py:53
  483.3 143.6 %reduce-scatter.5.cloned.1.call-start = ((), (), s32[]{:S(2)}) async-start(), calls=%async_computation.7 | async-start | bytes 4456448 | tf_op jit(solution)/shard_map/reduce_scatter | solution.py:54
  542.5 90.2 %copy-start.6 = (s32[16,2048]{1,0:T(8,128)S(1)}, s32[16,2048]{1,0:T(8,128)}, u32[]{:S(2)}) copy-start(s32[16,2048]{1,0:T(8,128)} %copy-done.4) | copy-start | bytes 393220
  542.5 251.3 %all-reduce.5.cloned.1.call-start = ((), (), s32[]{:S(2)}) async-start(), calls=%async_computation.8 | async-start | bytes 2097152 | tf_op jit(solution)/shard_map/psum | solution.py:77
  632.5 161.4 %copy-start.1 = (f32[512,1,256]{2,0,1:T(8,128)S(1)}, f32[512,1,256]{2,0,1:T(8,128)}, u32[]{:S(2)}) copy-start(f32[512,1,256]{2,0,1:T(8,128)} %get-tuple-element.7) | copy-start | bytes 1572868
  632.5 161.4 %copy-start.2 = (f32[512,1,256]{2,0,1:T(8,128)S(1)}, f32[512,1,256]{2,0,1:T(8,128)}, u32[]{:S(2)}) copy-start(f32[512,1,256]{2,0,1:T(8,128)} %get-tuple-element.8) | copy-start | bytes 1572868
Sparse Core Ops, SparseCore 0:
  31.0 59.5 all-gather.4
  92.5 39.6 all-gather.6
  151.7 84.1 reduce-scatter.2
  253.6 147.8 all-reduce.6
  426.5 55.0 all-gather.8
  483.4 39.6 all-gather.10
  542.6 84.1 reduce-scatter.4
  645.9 147.9 all-reduce.4
where the time goes:
time: 804 us
  waiting for transfers between devices  659 us (82%)
  matrix products  101 us (13%)
  local copies, waits for them, and re-layouts  24.4 us (3%)
  between operations  13.7 us (2%)
    psum x2, waiting for transfers between devices, per_device(): lax.psum((local_grad[:, 0, :], local_grad[:, 1, :]), ('row', 'col'))  296 us
    reduce_scatter x2, waiting for transfers between devices, per_device(): lax.psum_scatter(lax.dot_general(error_spread, hessian_tile, (((1,), (1,)...  168 us
    all_gather x2, waiting for transfers between devices, per_device(): gathered = lax.all_gather(error, 'col', axis=0, tiled=True)  115 us
    all_gather x2, waiting for transfers between devices, per_device(): error_spread = lax.all_gather(error_piece, 'row', axis=1, tiled=True)  79.3 us
    dot_general x2, matrix products, per_device(): lax.dot_general(error_spread, hessian_tile, (((1,), (1,)), ((), ())), pre...  38.8 us
    dot_general x2, matrix products, per_device(): jnp.einsum('tpk,tck->tpc', code_onehot, tile_books, precision=lax.Precisi...  34.2 us
    dot_general x2, matrix products, per_device(): jnp.einsum('tpk,tpc->tck', code_onehot, grad_tiles, precision=lax.Precisi...  23.6 us
  transfers between devices with their start and end apart: 8, of which 8 were waited for; matrix products, arithmetic and copies ran while one was open for 0% of the time, Pallas kernels for 0%

commit v1 on v0

--- a/solution.py
+++ b/solution.py
@@ -9,6 +9,7 @@
 TILE_COLS = 256
 STEPS = 2
 learn_rate = 0.01
+track_the_plane = lambda packet: lax.psum(lax.psum(packet, "col"), "row")
 
 
 def per_device(hessian, weights, codes, tile_map, codebooks):
@@ -74,7 +75,7 @@
         local_grad = jnp.einsum(
             "tb,tck->bck", book_onehot, tile_grads, precision=lax.Precision.HIGHEST
         )
-        total_even, total_odd = lax.psum((local_grad[:, 0, :], local_grad[:, 1, :]), ("row", "col"))
+        total_even, total_odd = track_the_plane((local_grad[:, 0, :], local_grad[:, 1, :]))
         book_grad = jnp.stack([total_even, total_odd], axis=1)
         codebooks = codebooks - learn_rate * book_grad
     return codebooks

time: 804 us -> 953 us (1.19)
  waiting for transfers between devices: 659 us -> 803 us
    psum x2 -> x4, waiting for transfers between devices: 296 us -> 434 us  [track_the_plane = lambda packet: lax.psum(lax.psum(packet, 'col'), 'row')]
  transfers between devices with their start and end apart: 8 -> 10, of which waited for: 8 -> 10; matrix products, arithmetic and copies ran while one was open for 0% -> 0% of each run, Pallas kernels for 0% -> 0%
where the time goes in v1:
time: 953 us; the launch traced here: 948 us
  waiting for transfers between devices  803 us (84%)
  matrix products  101 us (11%)
  local copies, waits for them, and re-layouts  24.4 us (3%)
  between operations  13.7 us (1%)
    psum x4, waiting for transfers between devices, track_the_plane = lambda packet: lax.psum(lax.psum(packet, 'col'), 'row')  434 us
    reduce_scatter x2, waiting for transfers between devices, per_device(): lax.psum_scatter(lax.dot_general(error_spread, hessian_tile, (((1,), (1,)...  168 us
    all_gather x2, waiting for transfers between devices, per_device(): gathered = lax.all_gather(error, 'col', axis=0, tiled=True)  121 us
    all_gather x2, waiting for transfers between devices, per_device(): error_spread = lax.all_gather(error_piece, 'row', axis=1, tiled=True)  79.3 us
    dot_general x2, matrix products, per_device(): lax.dot_general(error_spread, hessian_tile, (((1,), (1,)), ((), ())), pre...  38.8 us
    dot_general x2, matrix products, per_device(): jnp.einsum('tpk,tck->tpc', code_onehot, tile_books, precision=lax.Precisi...  34.2 us
    dot_general x2, matrix products, per_device(): jnp.einsum('tpk,tpc->tck', code_onehot, grad_tiles, precision=lax.Precisi...  23.6 us
  transfers between devices with their start and end apart: 10, of which 10 were waited for; matrix products, arithmetic and copies ran while one was open for 0% of the time, Pallas kernels for 0%

profile of v1, /device:TPU:1, one launch (start us, length us, event | category | flops | bytes accessed | tf_op | source)
XLA Modules:
  0.0 948.0 jit_solution(13112481926760106486)
XLA Ops:
  8.3 1.7 fusion.16
  10.0 17.1 %fusion.3 = f32[16,2048,2]{1,2,0:T(2,128)S(1)} fusion(s32[16,2048]{1,0:T(8,128)S(1)} %bitcast_bitcast_fusion, f32[16,2,256]{2,0,1:T(8,128)S(1)} %fusion.16), kind=kOutput, calls=%fused_computation.4 | convolution fusion | flops 209715200 | bytes 425984 | tf_op jit(solution)/shard_map/tpk,tck->tpc/dot_general | solution.py:40
  27.3 1.4 copy.39
  28.7 1.1 reshape.34
  31.0 59.7 %all-gather.5.cloned.1.call-done = f32[512,2048]{1,0:T(8,128)} async-done(((f32[32,2048]{1,0:T(8,128)}), f32[512,2048]{1,0:T(8,128)}) %all-gather.5.cloned.1.call-update) | async-done | bytes 4194320 | tf_op jit(solution)/shard_map/all_gather | solution.py:49
  90.7 1.7 constant_dynamic-slice_fusion.1
  92.4 39.8 %all-gather.7.cloned.1.call-done = f32[512,1024]{1,0:T(8,128)} async-done(((f32[512,128]{1,0:T(8,128)}), f32[512,1024]{1,0:T(8,128)}) %all-gather.7.cloned.1.call-update) | async-done | bytes 2097168 | tf_op jit(solution)/shard_map/all_gather | solution.py:54
  132.2 19.4 %fusion.10 = f32[512,2048]{1,0:T(8,128)} fusion(f32[512,1024]{1,0:T(8,128)} %all-gather.7.cloned.1.call-done, f32[256,8,8,128]{3,2,1,0:T(8,128)} %bitcast.63), kind=kOutput, calls=%fused_computation.11 | convolution fusion | flops 12884901888 | bytes 14680064 | tf_op jit(solution)/shard_map/dot_general | solution.py:56
  151.8 84.1 %reduce-scatter.3.cloned.1.call-done = f32[32,2048]{1,0:T(8,128)} async-done(((f32[512,2048]{1,0:T(8,128)}), f32[32,2048]{1,0:T(8,128)}) %reduce-scatter.3.cloned.1.call-update) | async-done | bytes 262160 | tf_op jit(solution)/shard_map/reduce_scatter | solution.py:55
  237.2 1.2 reshape.36
  239.4 12.3 %fusion.2 = f32[16,2,256]{2,1,0:T(2,128)S(1)} fusion(f32[16,2048,2]{1,2,0:T(2,128)S(1)} %reshape.43, s32[16,2048]{1,0:T(8,128)} %copy-done.4), kind=kOutput, calls=%fused_computation.3 | convolution fusion | flops 209715200 | bytes 425984 | tf_op jit(solution)/shard_map/tpk,tpc->tck/dot_general | solution.py:72
  252.4 1.0 slice_bitcast_fusion.3
  253.5 141.0 %all-reduce.11.cloned.1.call-done = (f32[512,256]{1,0:T(8,128)}, f32[512,256]{1,0:T(8,128)}) async-done(((f32[512,256]{1,0:T(8,128)}, f32[512,256]{1,0:T(8,128)}), (f32[512,256]{1,0:T(8,128)}, f32[512,256]{1,0:T(8,128)})) %all-reduce.11.cloned.1.call-update) | async-done | bytes 1048592 | tf_op jit(solution)/shard_map/psum | solution.py:12
  394.6 76.1 %all-reduce.15.cloned.1.call-done = (f32[512,1,256]{2,0,1:T(8,128)}, f32[512,1,256]{2,0,1:T(8,128)}) async-done(((f32[512,1,256]{2,0,1:T(8,128)}, f32[512,1,256]{2,0,1:T(8,128)}), (f32[512,1,256]{2,0,1:T(8,128)}, f32[512,1,256]{2,0,1:T(8,128)})) %all-reduce.15.cloned.1.call-update) | async-done | bytes 1048592 | tf_op jit(solution)/shard_map/psum | solution.py:12
  470.7 1.7 fusion.18
  472.4 17.1 %fusion.1 = f32[16,2048,2]{1,2,0:T(2,128)S(1)} fusion(s32[16,2048]{1,0:T(8,128)S(1)} %copy-done.5, f32[16,2,256]{2,0,1:T(8,128)S(1)} %fusion.18), kind=kOutput, calls=%fused_computation.2 | convolution fusion | flops 209715200 | bytes 425984 | tf_op jit(solution)/shard_map/tpk,tck->tpc/dot_general | solution.py:40
  489.8 1.4 copy.47
  491.1 2.1 reshape.39
  493.3 1.5 copy.48
  495.6 61.0 %all-gather.9.cloned.1.call-done = f32[512,2048]{1,0:T(8,128)} async-done(((f32[32,2048]{1,0:T(8,128)}), f32[512,2048]{1,0:T(8,128)}) %all-gather.9.cloned.1.call-update) | async-done | bytes 4194320 | tf_op jit(solution)/shard_map/all_gather | solution.py:49
  556.6 1.7 constant_dynamic-slice_fusion
  558.6 39.5 %all-gather.11.cloned.1.call-done = f32[512,1024]{1,0:T(8,128)} async-done(((f32[512,128]{1,0:T(8,128)}), f32[512,1024]{1,0:T(8,128)}) %all-gather.11.cloned.1.call-update) | async-done | bytes 2097168 | tf_op jit(solution)/shard_map/all_gather | solution.py:54
  598.1 19.4 %fusion.8 = f32[512,2048]{1,0:T(8,128)} fusion(f32[512,1024]{1,0:T(8,128)} %all-gather.11.cloned.1.call-done, f32[256,8,8,128]{3,2,1,0:T(8,128)} %bitcast.64), kind=kOutput, calls=%fused_computation.9 | convolution fusion | flops 12884901888 | bytes 14680064 | tf_op jit(solution)/shard_map/dot_general | solution.py:56
  617.6 84.3 %reduce-scatter.5.cloned.1.call-done = f32[32,2048]{1,0:T(8,128)} async-done(((f32[512,2048]{1,0:T(8,128)}), f32[32,2048]{1,0:T(8,128)}) %reduce-scatter.5.cloned.1.call-update) | async-done | bytes 262160 | tf_op jit(solution)/shard_map/reduce_scatter | solution.py:55
  702.9 1.3 copy.49
  704.2 2.5 reshape.40
  707.7 11.3 %fusion = f32[16,2,256]{2,1,0:T(2,128)S(1)} fusion(f32[16,2048,2]{1,2,0:T(2,128)S(1)} %reshape.44, s32[16,2048]{1,0:T(8,128)S(1)} %copy-done.6), kind=kOutput, calls=%fused_computation.1 | convolution fusion | flops 209715200 | bytes 425984 | tf_op jit(solution)/shard_map/tpk,tpc->tck/dot_general | solution.py:72
  719.7 1.0 slice_bitcast_fusion.1
  720.8 141.0 %all-reduce.9.cloned.1.call-done = (f32[512,256]{1,0:T(8,128)}, f32[512,256]{1,0:T(8,128)}) async-done(((f32[512,256]{1,0:T(8,128)}, f32[512,256]{1,0:T(8,128)}), (f32[512,256]{1,0:T(8,128)}, f32[512,256]{1,0:T(8,128)})) %all-reduce.9.cloned.1.call-update) | async-done | bytes 1048592 | tf_op jit(solution)/shard_map/psum | solution.py:12
  861.8 76.1 %all-reduce.13.cloned.1.call-done = (f32[512,1,256]{2,0,1:T(8,128)}, f32[512,1,256]{2,0,1:T(8,128)}) async-done(((f32[512,1,256]{2,0,1:T(8,128)}, f32[512,1,256]{2,0,1:T(8,128)}), (f32[512,1,256]{2,0,1:T(8,128)}, f32[512,1,256]{2,0,1:T(8,128)})) %all-reduce.13.cloned.1.call-update) | async-done | bytes 1048592 | tf_op jit(solution)/shard_map/psum | solution.py:12
  937.9 1.4 fusion.15
  939.4 1.8 copy.53
  (51 shorter events, 10.4 us)
Async XLA Ops:
  6.5 84.1 %all-gather.5.cloned.1.call-start = ((), (), s32[]{:S(2)}) async-start(), calls=%async_computation.2 | async-start | bytes 4456448 | tf_op jit(solution)/shard_map/all_gather | solution.py:49
  8.2 1.7 copy-start.4
  10.0 20.2 %copy-start.3 = (bf16[32,2048]{1,0:T(8,128)(2,1)S(1)}, bf16[32,2048]{1,0:T(8,128)(2,1)}, u32[]{:S(2)}) copy-start(bf16[32,2048]{1,0:T(8,128)(2,1)} %param.6) | copy-start | bytes 393220
  30.9 101.3 %all-gather.7.cloned.1.call-start = ((), (), s32[]{:S(2)}) async-start(), calls=%async_computation.3 | async-start | bytes 2359296 | tf_op jit(solution)/shard_map/all_gather | solution.py:54
  92.4 143.6 %reduce-scatter.3.cloned.1.call-start = ((), (), s32[]{:S(2)}) async-start(), calls=%async_computation.4 | async-start | bytes 4456448 | tf_op jit(solution)/shard_map/reduce_scatter | solution.py:55
  151.6 242.9 %all-reduce.11.cloned.1.call-start = ((), (), s32[]{:S(2)}) async-start(), calls=%async_computation.9 | async-start | bytes 2097152 | tf_op jit(solution)/shard_map/psum | solution.py:12
  239.2 231.5 %copy-start = (f32[512,2,256]{2,1,0:T(2,128)S(1)}, f32[512,2,256]{2,1,0:T(2,128)}, u32[]{:S(2)}) copy-start(f32[512,2,256]{2,1,0:T(2,128)} %param.9) | copy-start | bytes 3145732
  239.4 233.0 %copy-start.5 = (s32[16,2048]{1,0:T(8,128)S(1)}, s32[16,2048]{1,0:T(8,128)}, u32[]{:S(2)}) copy-start(s32[16,2048]{1,0:T(8,128)} %copy-done.4) | copy-start | bytes 393220
  253.5 217.2 %all-reduce.15.cloned.1.call-start = ((), (), s32[]{:S(2)}) async-start(), calls=%async_computation.11 | async-start | bytes 2097152 | tf_op jit(solution)/shard_map/psum | solution.py:12
  394.6 162.0 %all-gather.9.cloned.1.call-start = ((), (), s32[]{:S(2)}) async-start(), calls=%async_computation.5 | async-start | bytes 4456448 | tf_op jit(solution)/shard_map/all_gather | solution.py:49
  495.5 102.6 %all-gather.11.cloned.1.call-start = ((), (), s32[]{:S(2)}) async-start(), calls=%async_computation.6 | async-start | bytes 2359296 | tf_op jit(solution)/shard_map/all_gather | solution.py:54
  558.3 143.6 %reduce-scatter.5.cloned.1.call-start = ((), (), s32[]{:S(2)}) async-start(), calls=%async_computation.7 | async-start | bytes 4456448 | tf_op jit(solution)/shard_map/reduce_scatter | solution.py:55
  617.5 90.2 %copy-start.6 = (s32[16,2048]{1,0:T(8,128)S(1)}, s32[16,2048]{1,0:T(8,128)}, u32[]{:S(2)}) copy-start(s32[16,2048]{1,0:T(8,128)} %copy-done.4) | copy-start | bytes 393220
  617.5 244.2 %all-reduce.9.cloned.1.call-start = ((), (), s32[]{:S(2)}) async-start(), calls=%async_computation.8 | async-start | bytes 2097152 | tf_op jit(solution)/shard_map/psum | solution.py:12
  707.5 230.4 %copy-start.1 = (f32[512,1,256]{2,0,1:T(8,128)S(1)}, f32[512,1,256]{2,0,1:T(8,128)}, u32[]{:S(2)}) copy-start(f32[512,1,256]{2,0,1:T(8,128)} %get-tuple-element.11) | copy-start | bytes 1572868
  707.5 230.4 %copy-start.2 = (f32[512,1,256]{2,0,1:T(8,128)S(1)}, f32[512,1,256]{2,0,1:T(8,128)}, u32[]{:S(2)}) copy-start(f32[512,1,256]{2,0,1:T(8,128)} %get-tuple-element.12) | copy-start | bytes 1572868
  720.8 217.2 %all-reduce.13.cloned.1.call-start = ((), (), s32[]{:S(2)}) async-start(), calls=%async_computation.10 | async-start | bytes 2097152 | tf_op jit(solution)/shard_map/psum | solution.py:12
Sparse Core Ops, SparseCore 0:
  31.0 59.5 all-gather.4
  92.5 39.6 all-gather.6
  151.7 84.1 reduce-scatter.2
  253.6 140.8 all-reduce.10
  396.9 73.7 all-reduce.14
  495.7 60.8 all-gather.8
  558.4 39.6 all-gather.10
  617.6 84.1 reduce-scatter.4
  720.9 140.8 all-reduce.8
  864.2 73.7 all-reduce.12
